TPU v7x, 256 devices: a whole 4x4x8 slice. The times are simulated.
256 devices in a mesh: cont: 8 (over y, core), dev: 32 (over x, z).
Axes of the slice: x: 4, y: 4, z: 8, core: 2. Of those that a mesh axis runs over, the one named last changes fastest.
Arguments:
- station_values: bfloat16 [256, 128, 366], P(('cont', 'dev')), may hold values from -6 to 6
- krige_weights: bfloat16 [256, 128, 512], P(('cont', 'dev')), may hold values from -0.25 to 0.25
- inv_factor: bfloat16 [256, 128, 128], P(('cont', 'dev')), may hold values from -4 to 4
- cond_blocks: int32 [256, 4], P(('cont', 'dev')), may hold values from 0 to 255, as said below
- station_xy: bfloat16 [256, 2, 128], P(('cont', 'dev')), may hold values from 0 to 2
- cell_xy: float32 [2, 1048576], P(None, ('cont', 'dev')), may hold values from 0 to 2
- tile_blocks: int32 [1024, 16], P(('cont', 'dev')), may hold values from 0 to 255, as said below
- rain: float32 [60, 1048576], P(None, ('cont', 'dev')), may hold values from -6 to 6
Outputs:
- thresholds: bfloat16 [1048576, 366], P(('cont', 'dev'))
- exceed_share: float32 [1048576], P(('cont', 'dev'))
Inputs may be any that keep to these rules, and one draw needn't show every extreme that they name: `cond_blocks`: row b names 4 different blocks of b's continent c (blocks c * 32 to c * 32 + 31), never b itself. `tile_blocks`: row t names 16 different blocks, each of the continent of tile t or of the continent before it (continent c - 1, and 7 before 0); tile t lies in continent t // 128.
All inputs are finite; a program needn't handle non-finite values.
Results may differ from a plain program's by a relative error of at most 0.0069.
Values may be sent and summed in bfloat16 or wider, within the bound.
A program may use at most 64 MiB of HBM per device.

v0:
```python
import jax
import jax.numpy as jnp
from jax import lax
from jax.sharding import PartitionSpec as P

WIN = 60
WSTART = 150


sharpness = 4.0
cov_scale = 0.0625


def from_behind(block, axis, distance):
    devices = range(lax.axis_size(axis))
    route = [((i - distance) % len(devices), i) for i in devices]
    return lax.ppermute(block, axis, route)


def covariance(cell_x, cell_y, station_x, station_y, length):
    distance_sq = (cell_x[:, None] - station_x[None, :]) ** 2 + (
        cell_y[:, None] - station_y[None, :]
    ) ** 2
    return (jnp.exp(-jnp.sqrt(distance_sq + (length * 0.1) ** 2) / length) * cov_scale).astype(
        jnp.bfloat16
    )


def exceedance(threshold, rain_tile):
    window = jnp.roll(threshold, -WSTART, axis=1)[:, :WIN]
    return jnp.mean(jax.nn.sigmoid((rain_tile.T - window) * sharpness), axis=1)


def per_device(
    station_values, krige_weights, inv_factor, cond_blocks, station_xy, cell_xy, tile_blocks, rain
):
    group_size = lax.axis_size("dev")
    first_block = lax.axis_index("cont") * group_size
    local_cond = cond_blocks[0] - first_block
    block_rows = station_values.shape[1]
    day_count = station_values.shape[2]
    continent_values = lax.all_gather(station_values, "dev", axis=0, tiled=True)
    prior_rows = jnp.take(continent_values, local_cond, axis=0).reshape(-1, day_count)
    predicted = jnp.dot(krige_weights[0], prior_rows, preferred_element_type=jnp.float32)
    innovation = (station_values[0].astype(jnp.float32) - predicted).astype(jnp.bfloat16)
    whitened = jnp.dot(inv_factor[0], innovation, preferred_element_type=jnp.float32).astype(
        jnp.bfloat16
    )
    kweights = lax.dot_general(
        inv_factor[0], whitened, (((0,), (0,)), ((), ())), preferred_element_type=jnp.float32
    ).astype(jnp.bfloat16)[None]
    own_weights, own_coords = (
        lax.all_gather(kweights, "dev", axis=0, tiled=True),
        lax.all_gather(station_xy, "dev", axis=0, tiled=True),
    )
    prev_weights, prev_coords = from_behind((own_weights, own_coords), "cont", 1)
    cand_weights = jnp.concatenate([prev_weights, own_weights], axis=0)
    cand_coords = jnp.concatenate([prev_coords, own_coords], axis=0)
    in_continent = tile_blocks // group_size * group_size == first_block
    slots = jnp.where(in_continent, group_size + tile_blocks % group_size, tile_blocks % group_size)
    tile_count = tile_blocks.shape[0]
    tile_cells = cell_xy.shape[1] // tile_count
    cell_grid = jnp.transpose(cell_xy.reshape(2, tile_count, tile_cells), (1, 0, 2))
    rain_grid = jnp.transpose(rain.reshape(rain.shape[0], tile_count, tile_cells), (1, 0, 2))
    listed = slots.shape[1]
    length = 9.0 * (listed * block_rows) ** (-0.5)

    def one_tile(inputs):
        tile_slots, cell_coords, rain_tile = inputs
        chosen = jnp.take(cand_weights, tile_slots, axis=0).reshape(listed * block_rows, day_count)
        coords = jnp.take(cand_coords, tile_slots, axis=0).astype(jnp.float32)
        station_x = coords[:, 0, :].reshape(listed * block_rows)
        station_y = coords[:, 1, :].reshape(listed * block_rows)
        weights_tile = covariance(cell_coords[0], cell_coords[1], station_x, station_y, length)
        threshold = jnp.dot(weights_tile, chosen, preferred_element_type=jnp.float32)
        return (threshold.astype(jnp.bfloat16), exceedance(threshold, rain_tile))

    threshold_all, share_all = lax.map(one_tile, (slots, cell_grid, rain_grid))
    return (threshold_all.reshape(-1, day_count), share_all.reshape(-1))


def solution(mesh):
    placed = (
        P(("cont", "dev"), None, None),
        P(("cont", "dev"), None, None),
        P(("cont", "dev"), None, None),
        P(("cont", "dev"), None),
        P(("cont", "dev"), None, None),
        P(None, ("cont", "dev")),
        P(("cont", "dev"), None),
        P(None, ("cont", "dev")),
    )
    return jax.shard_map(
        per_device,
        mesh=mesh,
        in_specs=placed,
        out_specs=(P(("cont", "dev"), None), P(("cont", "dev"))),
        check_vma=False,
    )
```

profile of v0, /device:TPU:1, one launch (start us, length us, event | category | flops | bytes accessed | tf_op | source)
XLA Modules:
  0.0 311.6 jit_solution(2679706742689969512)
XLA Ops:
  9.3 80.7 %all-gather.4.cloned.1.call-done = bf16[32,128,366]{1,2,0:T(8,128)(2,1)} async-done(((bf16[1,128,366]{1,2,0:T(8,128)(2,1)}), bf16[32,128,366]{1,2,0:T(8,128)(2,1)}) %all-gather.4.cloned.1.call-update) | async-done | bytes 2998288 | tf_op jit(solution)/shard_map/all_gather | solution.py:42
  90.1 2.5 gather_fusion.2
  92.9 1.2 fusion.13
  94.1 1.0 fusion.14
  95.1 76.2 %all-gather.6.cloned.1.call-done = bf16[4096,366]{0,1:T(8,128)(2,1)} async-done(((bf16[128,366]{0,1:T(8,128)(2,1)}), bf16[4096,366]{0,1:T(8,128)(2,1)}) %all-gather.6.cloned.1.call-update) | async-done | bytes 2998288 | tf_op jit(solution)/shard_map/all_gather | solution.py:53
  171.3 2.6 copy.23
  174.5 4.2 %collective-permute-start.1 = (bf16[32,128,366]{1,0,2:T(8,128)(2,1)S(1)}, bf16[32,128,366]{1,0,2:T(8,128)(2,1)}, u32[]{:S(2)}, u32[]{:S(2)}) collective-permute-start(bf16[32,128,366]{1,0,2:T(8,128)(2,1)S(1)} %slice_bitcast_fusion), channel_id=1, source_target_pairs={{224,0},{0,32},{32,64},{64,96},{96,128},{128,160},{160,192},{192,2... | collective-permute-start | bytes 8994824 | tf_op jit(solution)/shard_map/ppermute | solution.py:17
  178.7 35.2 %all_gather.9 = bf16[32,2,128]{2,1,0:T(2,128)(2,1)S(1)} all-gather(bf16[1,2,128]{2,1,0:T(2,128)(2,1)S(1)} %copy-done.3), channel_id=1, replica_groups=mesh['cont'=8,'dev'=32] {'dev'}, dimensions={0}, use_global_device_ids=true | all-gather | bytes 16896 | tf_op jit(solution)/shard_map/all_gather | solution.py:54
  213.9 3.8 %collective-permute-start = (bf16[32,2,128]{2,1,0:T(2,128)(2,1)S(1)}, bf16[32,2,128]{2,1,0:T(2,128)(2,1)S(1)}, u32[]{:S(2)}, u32[]{:S(2)}) collective-permute-start(bf16[32,2,128]{2,1,0:T(2,128)(2,1)S(1)} %all_gather.9), channel_id=1, source_target_pairs={{224,0},{0,32},{32,64},{64,96},{96,128},{128,160},{160,192},{192,2... | collective-permute-start | bytes 49160 | tf_op jit(solution)/shard_map/ppermute | solution.py:17
  217.8 2.9 reshape.135
  220.7 6.6 %pad_maximum_fusion = bf16[64,128,366]{1,0,2:T(8,128)(2,1)} fusion(bf16[32,128,366]{1,0,2:T(8,128)(2,1)S(1)} %slice_bitcast_fusion, bf16[32,128,366]{1,0,2:T(8,128)(2,1)} %collective-permute-done.1), kind=kLoop, calls=%fused_computation.31 | loop fusion | flops 11993088 | bytes 11993088 | tf_op jit(solution)/shard_map/concatenate | solution.py:57
  227.3 9.0 %copy.19 = bf16[64,128,366]{2,1,0:T(8,128)(2,1)} copy(bf16[64,128,366]{1,0,2:T(8,128)(2,1)} %pad_maximum_fusion) | data formatting | bytes 11993088 | tf_op jit(solution)/shard_map/while | solution.py:78
  236.3 59.5 %while.12 = (s32[]{:T(128)}, bf16[4,1024,366]{1,2,0:T(8,128)(2,1)}, f32[4,1024]{1,0:T(4,128)S(1)}, f32[4,2,1024]{2,1,0:T(2,128)}, s32[4,16]{1,0:T(4,128)S(1)}, /...) while((s32[]{:T(128)}, bf16[4,1024,366]{1,2,0:T(8,128)(2,1)}, ...), condition=%wide.region_2.3_spmd, body=%wide.region_0.0_spmd.sunk | while | flops 1557589120 | bytes 10875969 | solution.py:78
  237.0 3.7 %gather_fusion = bf16[16,128,366]{2,1,0:T(8,128)(2,1)S(1)} fusion(bf16[64,128,366]{2,1,0:T(8,128)(2,1)} %get-tuple-element.174, s32[1024]{0:T(1024)S(1)} %pad_clamp_fusion.3), kind=kCustom, calls=%fused_computation.1.clone.1 | custom fusion | bytes 2998336 | tf_op jit(solution)/shard_map/while/body/eval_jaxpr/jit(_take)/gather | solution.py:70
  241.4 0.8 constant_dynamic-slice_fusion.6
  242.2 7.3 %bitcast_dynamic-update-slice_fusion.2 = (bf16[4,1024,366]{1,2,0:T(8,128)(2,1)}, f32[1024,366]{0,1:T(8,128)S(1)}) fusion(bf16[4,1024,366]{1,2,0:T(8,128)(2,1)} %get-tuple-element.158, s32[]{:T(128)} %get-tuple-element.157, bf16[2048,366]{1,0:T(8,128)(2,1)S(1)} %bitcast_select_fusion.2, f32[2048]{0:T(1024)S(1)} %bitcast.109, f32[1024]{0:T(1024)S(1)} %bitcast.111, ...), kind=kOutput, calls=%fused_computation.6.clone.1 | convolution fusion | flops 1556461568 | bytes 3777024 | tf_op jit(solution)/shard_map/while/body/eval_jaxpr/dot_general | solution.py:75
  249.5 1.5 constant_dynamic-slice_fusion.7
  251.9 3.7 %gather_fusion = bf16[16,128,366]{2,1,0:T(8,128)(2,1)S(1)} fusion(bf16[64,128,366]{2,1,0:T(8,128)(2,1)} %get-tuple-element.174, s32[1024]{0:T(1024)S(1)} %pad_clamp_fusion.3), kind=kCustom, calls=%fused_computation.1.clone.1 | custom fusion | bytes 2998336 | tf_op jit(solution)/shard_map/while/body/eval_jaxpr/jit(_take)/gather | solution.py:70
  256.3 0.8 constant_dynamic-slice_fusion.6
  257.1 7.3 %bitcast_dynamic-update-slice_fusion.2 = (bf16[4,1024,366]{1,2,0:T(8,128)(2,1)}, f32[1024,366]{0,1:T(8,128)S(1)}) fusion(bf16[4,1024,366]{1,2,0:T(8,128)(2,1)} %get-tuple-element.158, s32[]{:T(128)} %get-tuple-element.157, bf16[2048,366]{1,0:T(8,128)(2,1)S(1)} %bitcast_select_fusion.2, f32[2048]{0:T(1024)S(1)} %bitcast.109, f32[1024]{0:T(1024)S(1)} %bitcast.111, ...), kind=kOutput, calls=%fused_computation.6.clone.1 | convolution fusion | flops 1556461568 | bytes 3777024 | tf_op jit(solution)/shard_map/while/body/eval_jaxpr/dot_general | solution.py:75
  264.4 1.5 constant_dynamic-slice_fusion.7
  266.8 3.7 %gather_fusion = bf16[16,128,366]{2,1,0:T(8,128)(2,1)S(1)} fusion(bf16[64,128,366]{2,1,0:T(8,128)(2,1)} %get-tuple-element.174, s32[1024]{0:T(1024)S(1)} %pad_clamp_fusion.3), kind=kCustom, calls=%fused_computation.1.clone.1 | custom fusion | bytes 2998336 | tf_op jit(solution)/shard_map/while/body/eval_jaxpr/jit(_take)/gather | solution.py:70
  271.2 0.8 constant_dynamic-slice_fusion.6
  272.0 7.3 %bitcast_dynamic-update-slice_fusion.2 = (bf16[4,1024,366]{1,2,0:T(8,128)(2,1)}, f32[1024,366]{0,1:T(8,128)S(1)}) fusion(bf16[4,1024,366]{1,2,0:T(8,128)(2,1)} %get-tuple-element.158, s32[]{:T(128)} %get-tuple-element.157, bf16[2048,366]{1,0:T(8,128)(2,1)S(1)} %bitcast_select_fusion.2, f32[2048]{0:T(1024)S(1)} %bitcast.109, f32[1024]{0:T(1024)S(1)} %bitcast.111, ...), kind=kOutput, calls=%fused_computation.6.clone.1 | convolution fusion | flops 1556461568 | bytes 3777024 | tf_op jit(solution)/shard_map/while/body/eval_jaxpr/dot_general | solution.py:75
  279.3 1.5 constant_dynamic-slice_fusion.7
  281.7 3.7 %gather_fusion = bf16[16,128,366]{2,1,0:T(8,128)(2,1)S(1)} fusion(bf16[64,128,366]{2,1,0:T(8,128)(2,1)} %get-tuple-element.174, s32[1024]{0:T(1024)S(1)} %pad_clamp_fusion.3), kind=kCustom, calls=%fused_computation.1.clone.1 | custom fusion | bytes 2998336 | tf_op jit(solution)/shard_map/while/body/eval_jaxpr/jit(_take)/gather | solution.py:70
  286.1 0.8 constant_dynamic-slice_fusion.6
  286.9 7.3 %bitcast_dynamic-update-slice_fusion.2 = (bf16[4,1024,366]{1,2,0:T(8,128)(2,1)}, f32[1024,366]{0,1:T(8,128)S(1)}) fusion(bf16[4,1024,366]{1,2,0:T(8,128)(2,1)} %get-tuple-element.158, s32[]{:T(128)} %get-tuple-element.157, bf16[2048,366]{1,0:T(8,128)(2,1)S(1)} %bitcast_select_fusion.2, f32[2048]{0:T(1024)S(1)} %bitcast.109, f32[1024]{0:T(1024)S(1)} %bitcast.111, ...), kind=kOutput, calls=%fused_computation.6.clone.1 | convolution fusion | flops 1556461568 | bytes 3777024 | tf_op jit(solution)/shard_map/while/body/eval_jaxpr/dot_general | solution.py:75
  294.1 1.5 constant_dynamic-slice_fusion.7
  295.8 4.2 %copy.33 = bf16[4,1024,366]{1,0,2:T(4,128)(2,1)S(1)} copy(bf16[4,1024,366]{1,2,0:T(8,128)(2,1)} %get-tuple-element.45) | data formatting | bytes 5996544 | tf_op jit(solution)/shard_map/while | solution.py:78
  300.0 1.2 pad.7
  301.2 3.0 copy.24
  (69 shorter events, 10.1 us)
Async XLA Ops:
  7.2 85.7 %copy-start = (bf16[1,128,512]{2,1,0:T(8,128)(2,1)S(1)}, bf16[1,128,512]{2,1,0:T(8,128)(2,1)}, u32[]{:S(2)}) copy-start(bf16[1,128,512]{2,1,0:T(8,128)(2,1)} %param.11) | copy-start | bytes 393220
  7.2 86.9 %copy-start.1 = (bf16[1,128,128]{2,1,0:T(8,128)(2,1)S(1)}, bf16[1,128,128]{2,1,0:T(8,128)(2,1)}, u32[]{:S(2)}) copy-start(bf16[1,128,128]{2,1,0:T(8,128)(2,1)} %param.12) | copy-start | bytes 98308
  7.2 82.9 %all-gather.4.cloned.1.call-start = ((), (), s32[]{:S(2)}) async-start(), calls=%async_computation | async-start | bytes 3108864 | tf_op jit(solution)/shard_map/all_gather | solution.py:42
  7.9 163.4 %all-gather.6.cloned.1.call-start = ((), (), s32[]{:S(2)}) async-start(), calls=%async_computation.1 | async-start | bytes 3108864 | tf_op jit(solution)/shard_map/all_gather | solution.py:53
  174.0 4.8 %copy-start.3 = (bf16[1,2,128]{2,1,0:T(2,128)(2,1)S(1)}, bf16[1,2,128]{2,1,0:T(2,128)(2,1)}, u32[]{:S(2)}) copy-start(bf16[1,2,128]{2,1,0:T(2,128)(2,1)} %param.14) | copy-start | bytes 1540
  174.0 43.7 %copy-start.2 = (s32[4,16]{1,0:T(4,128)S(1)}, s32[4,16]{1,0:T(4,128)}, u32[]{:S(2)}) copy-start(s32[4,16]{1,0:T(4,128)} %param.16) | copy-start | bytes 772
  174.5 46.2 %collective-permute-start.1 = (bf16[32,128,366]{1,0,2:T(8,128)(2,1)S(1)}, bf16[32,128,366]{1,0,2:T(8,128)(2,1)}, u32[]{:S(2)}, u32[]{:S(2)}) collective-permute-start(bf16[32,128,366]{1,0,2:T(8,128)(2,1)S(1)} %slice_bitcast_fusion), channel_id=1, source_target_pairs={{224,0},{0,32},{32,64},{64,96},{96,128},{128,160},{160,192},{192,2... | collective-permute-start | bytes 8994824 | tf_op jit(solution)/shard_map/ppermute | solution.py:17
  213.9 6.8 %collective-permute-start = (bf16[32,2,128]{2,1,0:T(2,128)(2,1)S(1)}, bf16[32,2,128]{2,1,0:T(2,128)(2,1)S(1)}, u32[]{:S(2)}, u32[]{:S(2)}) collective-permute-start(bf16[32,2,128]{2,1,0:T(2,128)(2,1)S(1)} %all_gather.9), channel_id=1, source_target_pairs={{224,0},{0,32},{32,64},{64,96},{96,128},{128,160},{160,192},{192,2... | collective-permute-start | bytes 49160 | tf_op jit(solution)/shard_map/ppermute | solution.py:17
Sparse Core Ops, SparseCore 0:
  10.6 79.3 all-gather.3
  95.2 76.0 all-gather.5
where the time goes:
time: 313 us; the launch traced here: 312 us
  waiting for transfers between devices  158 us (50%)
  local copies, waits for them, and re-layouts  53.3 us (17%)
  blocking collectives  35.2 us (11%)
  matrix products  31.3 us (10%)
  between operations  14.2 us (5%)
  other arithmetic  11.5 us (4%)
  starting transfers between devices  8.09 us (3%)
    all_gather x1, waiting for transfers between devices, per_device(): continent_values = lax.all_gather(station_values, 'dev', axis=0, tiled=True)  80.7 us
    all_gather x1, waiting for transfers between devices, per_device(): lax.all_gather(kweights, 'dev', axis=0, tiled=True)  76.2 us
    all_gather x1, blocking collectives, per_device(): lax.all_gather(station_xy, 'dev', axis=0, tiled=True)  35.2 us
    dot_general x4, matrix products, one_tile(): jnp.dot(weights_tile, chosen, preferred_element_type=jnp.float32)  29.1 us
    gather x4, local copies, waits for them, and re-layouts, one_tile(): jnp.take(cand_weights, tile_slots, axis=0)  14.7 us
    while x2, local copies, waits for them, and re-layouts, per_device(): threshold_all, share_all = lax.map(one_tile, (slots, cell_grid, rain_grid))  13.1 us
    ppermute x2, starting transfers between devices, from_behind(): return lax.ppermute(block, axis, route)  8.02 us
    unnamed x12, local copies, waits for them, and re-layouts  7.38 us
  transfers between devices with their start and end apart: 4, of which 2 were waited for; matrix products, arithmetic and copies ran while one was open for 1% of the time, Pallas kernels for 0%

commit v1 on v0

v1 whole, which is shorter than its diff:
```python
import functools
import math

import jax
import jax.numpy as jnp
from jax import lax
from jax.experimental import pallas as pl
from jax.experimental.pallas import tpu as pltpu
from jax.sharding import PartitionSpec as P

MESH = pl.DeviceIdType.MESH
BF16 = jnp.bfloat16
F32 = jnp.float32

XS, ZS = 4, 8
GROUP = XS * ZS
CONTS = 8
BS = 128
HALF = 64
QUARTER = 32
DAYS = 366
COLS = 384
NCOND = 4
LISTED = 16
STATIONS = LISTED * BS
TILES = 4
TILE = 1024
CELLS = TILES * TILE
WIN = 60
WSTART = 150
WLANE = WSTART // 128 * 128
WROW = (WSTART - WLANE) // 8 * 8
WOFF = WSTART - WLANE - WROW
WROWS = -(-(WOFF + WIN) // 8) * 8
LENGTH = 9.0 * STATIONS**-0.5
SCALE = math.log2(math.e) / LENGTH
NUGGET = (LENGTH * 0.1 * SCALE) ** 2
CHUNK = 512


class Place:
    def __init__(self):
        dev = lax.axis_index("dev")
        cont = lax.axis_index("cont")
        self.dev, self.cont = dev, cont
        self.x, self.z = dev // ZS, dev % ZS
        self.xs = [self.x, self.at_x(-1), self.at_x(1), self.at_x(2)]
        self.zs = [self.z] + [self.at_z(d) for s in (1, 2, 3) for d in (-s, s)] + [self.at_z(4)]
        self.xl, self.xr = self.xs[1] * ZS + self.z, self.xs[2] * ZS + self.z
        self.zl, self.zr = self.x * ZS + self.zs[1], self.x * ZS + self.zs[2]
        self.ahead = lax.rem(cont + 1, CONTS)
        self.behind = lax.rem(cont + CONTS - 1, CONTS)
        self.even = lax.rem(cont, 2) == 0

    def at_x(self, step):
        return lax.rem(self.x + (step + XS), XS)

    def at_z(self, step):
        return lax.rem(self.z + (step + ZS), ZS)


def remote(src, dst, send, recv, **device):
    return pltpu.make_async_remote_copy(
        src_ref=src, dst_ref=dst, send_sem=send, recv_sem=recv, device_id=device, device_id_type=MESH
    )


class Gather:
    def __init__(self, place, buf, send, recv):
        self.p, self.buf, self.send, self.recv = place, buf, send, recv

    def push(self, slot, sem, dev, rows=None):
        ref = self.buf.at[slot] if rows is None else self.buf.at[slot, pl.ds(rows, QUARTER)]
        remote(ref, ref, self.send, self.recv.at[sem], dev=dev).start()

    def arrived(self, slot, sem, rows=None):
        ref = self.buf.at[slot] if rows is None else self.buf.at[slot, pl.ds(rows, QUARTER)]
        remote(ref, ref, self.send, self.recv.at[sem], dev=self.p.dev).wait_recv()

    def sent(self):
        ref = self.buf.at[pl.ds(0, GROUP - 1)]
        remote(ref, ref, self.send, self.recv.at[0], dev=self.p.dev).wait_send()


class GatherA(Gather):
    def slot(self, z, x):
        return z * XS + x

    def zsem(self, s, way, j):
        return 4 + ((s - 1) * 2 + way) * XS + j

    def spread_z(self, j):
        p = self.p
        slot = self.slot(p.z, p.xs[j])
        self.push(slot, self.zsem(1, 0, j), p.zr)
        self.push(slot, self.zsem(1, 1, j), p.zl)

    def start(self):
        p = self.p
        own = self.slot(p.z, p.x)
        self.push(own, 0, p.xr)
        self.push(own, 1, p.xl)
        self.spread_z(0)

    def round(self, r):
        p = self.p
        if r == 1:
            left, right = self.slot(p.z, p.xs[1]), self.slot(p.z, p.xs[2])
            self.arrived(left, 0)
            self.push(left, 2, p.xr, 0)
            self.spread_z(1)
            self.arrived(right, 1)
            self.push(right, 3, p.xl, QUARTER)
            self.spread_z(2)
        if r == 2:
            far = self.slot(p.z, p.xs[3])
            self.arrived(far, 2, 0)
            self.arrived(far, 3, QUARTER)
            self.spread_z(3)
        for j, hop in enumerate((0, 1, 1, 2)):
            s = r - hop
            if 1 <= s <= 3:
                left, right = self.slot(p.at_z(-s), p.xs[j]), self.slot(p.at_z(s), p.xs[j])
                self.arrived(left, self.zsem(s, 0, j))
                if s < 3 or j % 2 == 0:
                    self.push(left, self.zsem(s + 1, 0, j), p.zr)
                self.arrived(right, self.zsem(s, 1, j))
                if s < 3 or j % 2 == 1:
                    self.push(right, self.zsem(s + 1, 1, j), p.zl)
            if s == 4:
                self.arrived(self.slot(p.at_z(4), p.xs[j]), self.zsem(4, j % 2, j))


A_SEMS = 4 + 4 * 2 * XS


class GatherB(Gather):
    def slot(self, x, z):
        return x * ZS + z

    def spread_x(self, i):
        p = self.p
        slot = self.slot(p.x, p.zs[i])
        self.push(slot, 8 + i, p.xr)
        self.push(slot, 16 + i, p.xl)

    def start(self):
        p = self.p
        own = self.slot(p.x, p.z)
        self.push(own, 0, p.zr)
        self.push(own, 1, p.zl)
        self.spread_x(0)

    def pass_x(self, i):
        p = self.p
        left, right = self.slot(p.xs[1], p.zs[i]), self.slot(p.xs[2], p.zs[i])
        self.arrived(left, 8 + i)
        if i in (0, 7):
            self.push(left, 24 + i, p.xr, 0)
        elif i % 2:
            self.push(left, 24 + i, p.xr)
        self.arrived(right, 16 + i)
        if i in (0, 7):
            self.push(right, 32 + i, p.xl, QUARTER)
        elif i % 2 == 0:
            self.push(right, 32 + i, p.xl)

    def end_x(self, i):
        p = self.p
        far = self.slot(p.xs[3], p.zs[i])
        if i in (0, 7):
            self.arrived(far, 24 + i, 0)
            self.arrived(far, 32 + i, QUARTER)
        elif i % 2:
            self.arrived(far, 24 + i)
        else:
            self.arrived(far, 32 + i)

    def round(self, r):
        p = self.p
        if 1 <= r <= 3:
            left, right = self.slot(p.x, p.at_z(-r)), self.slot(p.x, p.at_z(r))
            self.arrived(left, 2 * r - 2)
            self.push(left, 2 * r, p.zr, 0 if r == 3 else None)
            self.spread_x(2 * r - 1)
            self.arrived(right, 2 * r - 1)
            self.push(right, 2 * r + 1, p.zl, QUARTER if r == 3 else None)
            self.spread_x(2 * r)
        if r == 4:
            far = self.slot(p.x, p.zs[7])
            self.arrived(far, 6, 0)
            self.arrived(far, 7, QUARTER)
            self.spread_x(7)
        for s, members in enumerate(((0,), (1, 2), (3, 4), (5, 6), (7,))):
            for i in members:
                if r == s + 1:
                    self.pass_x(i)
                if r == s + 2:
                    self.end_x(i)


B_SEMS = 40


def dot(a, b, dims=((1,), (0,))):
    return lax.dot_general(a, b, (dims, ((), ())), preferred_element_type=F32)


def kernel(
    cond, tiles, sv, weights, factor, xy, cells, rain,
    out, share,
    sva, svb, kwa, kwb, coords, cellx, celly, rain_raw, rain_win, prior, cov, chosen,
    rain_sem,
    c_send, c_recv, cz_send, cc_send,
    sa_send, sa_recv, sb_send, sb_recv,
    ka_send, ka_recv, kb_send, kb_recv, kp_send, kp_recv,
    fa_send, fa_recv, fb_send, fb_recv, inj_send, inj_recv,
):
    p = Place()
    rain_copy = pltpu.make_async_copy(rain, rain_raw, rain_sem)
    rain_copy.start()

    ga = GatherA(p, sva, sa_send, sa_recv)
    gb = GatherB(p, svb, sb_send, sb_recv)
    slot_a, slot_b = ga.slot(p.z, p.x), gb.slot(p.x, p.z)

    barrier = pltpu.get_barrier_semaphore()
    x_peers = [p.at_x(s) * ZS + p.z for s in (1, 2, 3)]
    z_peers = [p.x * ZS + p.at_z(s) for s in range(1, ZS)]
    for peer in x_peers + z_peers:
        pl.semaphore_signal(barrier, inc=1, device_id={"dev": peer}, device_id_type=MESH)
    pl.semaphore_signal(barrier, inc=1, device_id={"cont": p.behind}, device_id_type=MESH)

    tail = jnp.zeros((HALF, COLS - DAYS), BF16)
    sva[slot_a] = jnp.concatenate([sv[0, :HALF, :], tail], axis=1)
    svb[slot_b] = jnp.concatenate([sv[0, HALF:, :], tail], axis=1)
    coords[1, slot_a] = jnp.concatenate(
        [xy[0].astype(F32) * SCALE, jnp.zeros((6, BS), F32)], axis=0
    )
    pl.semaphore_wait(barrier, XS + ZS - 1)

    def coord_x(s):
        ref = coords.at[1, slot_a]
        return remote(ref, ref, c_send, c_recv.at[s], dev=x_peers[s - 1])

    for s in (1, 2, 3):
        coord_x(s).start()
    ga.start()
    gb.start()

    def place_cells(first, last):
        def one(c, carry):
            lanes = pl.ds(pl.multiple_of(c * 128, 128), 128)
            for row, held in ((0, cellx), (1, celly)):
                line = cells[row : row + 1, lanes] * SCALE
                held[lanes, :] = jnp.transpose(jnp.broadcast_to(line, (128, 128)))
            return carry

        lax.fori_loop(first, last, one, 0)

    place_cells(0, 8)

    for s in (1, 2, 3):
        ref = coords.at[1, p.z * XS + p.at_x(-s)]
        remote(ref, ref, c_send, c_recv.at[s], dev=p.dev).wait_recv()
    for s in range(1, ZS):
        ref = coords.at[1, pl.ds(p.z * XS, XS)]
        remote(ref, ref, cz_send, c_recv.at[3 + s], dev=z_peers[s - 1]).start()

    ga.round(1)
    gb.round(1)
    place_cells(8, 20)

    for s in range(1, ZS):
        ref = coords.at[1, pl.ds(p.at_z(-s) * XS, XS)]
        remote(ref, ref, cz_send, c_recv.at[3 + s], dev=p.dev).wait_recv()
    coord_ahead = remote(coords.at[1], coords.at[0], cc_send, c_recv.at[0], cont=p.ahead)
    coord_ahead.start()

    ga.round(2)
    gb.round(2)
    place_cells(20, CELLS // 128)
    rain_copy.wait()
    rain_win[...] = jnp.zeros_like(rain_win)
    rain_win[WOFF : WOFF + WIN, :] = rain_raw[...]
    coord_ahead.wait_recv()

    def listed(t, k):
        block = tiles[t, k]
        own = jnp.where(block // GROUP == p.cont, 1, 0)
        dev = block % GROUP
        return own, dev % ZS * XS + dev // ZS, dev

    def cover(first, last):
        def one(g, carry):
            t, k = g // LISTED, g % LISTED
            own, at, _ = listed(t, k)
            sx, sy = coords[own, at, 0:1, :], coords[own, at, 1:2, :]
            lanes = pl.ds(pl.multiple_of(k * BS, BS), BS)

            def part(c, carry):
                rows = pl.ds(pl.multiple_of(t * TILE + c * 256, 256), 256)
                dx = cellx[rows, :] - sx
                dy = celly[rows, :] - sy
                square = dx * dx + dy * dy + NUGGET
                cov[rows, lanes] = jnp.exp2(-4.0 - square * lax.rsqrt(square)).astype(BF16)
                return carry

            return lax.fori_loop(0, TILE // 256, part, carry)

        lax.fori_loop(first, last, one, 0)

    cover(0, 3)
    done = 3
    for r in (3, 4, 5, 6):
        ga.round(r)
        cover(done, done + 4)
        gb.round(r)
        cover(done + 4, done + 8)
        done += 8

    for k in range(NCOND):
        dev = cond[0, k] % GROUP
        prior[k * BS : k * BS + HALF, :] = sva[dev % ZS * XS + dev // ZS]
        prior[k * BS + HALF : (k + 1) * BS, :] = svb[dev]
    predicted = dot(weights[0], prior[...])
    values = jnp.concatenate([sva[slot_a], svb[slot_b]], axis=0).astype(F32)
    innovation = (values - predicted).astype(BF16)
    whitened = dot(factor[0], innovation).astype(BF16)
    kweights = dot(factor[0], whitened, ((0,), (0,))).astype(BF16)
    kwa[1, slot_a] = kweights[:HALF]
    kwb[1, slot_b] = kweights[HALF:]

    ka = GatherA(p, kwa.at[1], ka_send, ka_recv)
    kb = GatherB(p, kwb.at[1], kb_send, kb_recv)
    kp = GatherB(p, kwb.at[0], kp_send, kp_recv)

    def inject():
        return remote(
            kwb.at[1, slot_b], kwb.at[0, slot_b], inj_send, inj_recv, cont=p.ahead
        )

    def ahead_a(i):
        part = pl.ds(p.zs[i] * XS, XS)
        return remote(kwa.at[1, part], kwa.at[0, part], fa_send, fa_recv.at[i], cont=p.ahead)

    def ahead_b(j):
        part = pl.ds(p.xs[j] * ZS, ZS)
        return remote(kwb.at[1, part], kwb.at[0, part], fb_send, fb_recv.at[j], cont=p.ahead)

    odd = jnp.logical_not(p.even)

    @pl.when(odd)
    def _():
        inject().start()

    ka.start()
    kb.start()
    left = TILES * LISTED - done
    spans = [done + left * i // 10 for i in range(11)]

    @pl.when(p.even)
    def _():
        inject().wait_recv()
        kp.start()

    cover(spans[0], spans[1])
    for r in range(1, 8):
        if r <= 6:
            ka.round(r)
            if r >= 2:
                for i in ((0,), (1, 2), (3, 4), (5, 6), (7,))[r - 2]:
                    ahead_a(i).start()
            if r <= 4:
                cover(spans[2 * r - 1], spans[2 * r])
            kb.round(r)

        @pl.when(p.even)
        def _(r=r):
            if r >= 2:
                kp.round(r - 1)
            for j in {4: (0,), 5: (1, 2), 6: (3,)}.get(r, ()):
                ahead_b(j).start()

        if r <= 4:
            cover(spans[2 * r], spans[2 * r + 1])
    cover(spans[9], spans[10])

    for i in range(ZS):
        ahead_a(i).wait_recv()

    @pl.when(odd)
    def _():
        for j in range(XS):
            ahead_b(j).wait_recv()

    for t in range(TILES):

        def choose(k, carry):
            own, at, dev = listed(t, k)
            chosen[pl.ds(pl.multiple_of(k * BS, BS), HALF), :] = kwa[own, at]
            chosen[pl.ds(pl.multiple_of(k * BS + HALF, HALF), HALF), :] = kwb[own, dev]
            return carry

        lax.fori_loop(0, LISTED, choose, 0)

        def part(c, carry):
            rows = pl.ds(pl.multiple_of(t * TILE + c * CHUNK, CHUNK), CHUNK)
            full = dot(cov[rows, :], chosen[...])
            out[rows, :] = full[:, :DAYS].astype(BF16)
            window = jnp.transpose(full[:, WLANE : WLANE + 128])[WROW : WROW + WROWS, :]
            soft = jnp.tanh((rain_win[:, rows] - window) * 2.0)
            row = lax.broadcasted_iota(jnp.int32, soft.shape, 0)
            soft = jnp.where((row >= WOFF) & (row < WOFF + WIN), soft, 0.0)
            total = jnp.sum(soft, axis=0, keepdims=True)
            share[:, rows] = total * (0.5 / WIN) + 0.5
            return carry

        lax.fori_loop(0, TILE // CHUNK, part, 0)

    ga.sent()
    gb.sent()
    ka.sent()
    kb.sent()
    ref = coords.at[1, pl.ds(0, 3)]
    remote(ref, ref, c_send, c_recv.at[0], dev=p.dev).wait_send()
    ref = coords.at[1, pl.ds(0, XS * (ZS - 1))]
    remote(ref, ref, cz_send, c_recv.at[0], dev=p.dev).wait_send()
    coord_ahead.wait_send()
    ref = kwa.at[1]
    remote(ref, ref, fa_send, fa_recv.at[0], dev=p.dev).wait_send()

    @pl.when(odd)
    def _():
        inject().wait_send()

    @pl.when(p.even)
    def _():
        kp.sent()
        ref = kwb.at[1]
        remote(ref, ref, fb_send, fb_recv.at[0], dev=p.dev).wait_send()


def per_device(sv, weights, factor, cond, xy, cells, tiles, rain):
    dma = pltpu.SemaphoreType.DMA
    vmem, smem = pl.BlockSpec(memory_space=pltpu.VMEM), pl.BlockSpec(memory_space=pltpu.SMEM)
    thresholds, share = pl.pallas_call(
        kernel,
        out_shape=(
            jax.ShapeDtypeStruct((CELLS, DAYS), BF16),
            jax.ShapeDtypeStruct((1, CELLS), F32),
        ),
        in_specs=[smem, smem, vmem, vmem, vmem, vmem, vmem, pl.BlockSpec(memory_space=pl.ANY)],
        out_specs=(vmem, vmem),
        scratch_shapes=[
            pltpu.VMEM((GROUP, HALF, COLS), BF16),
            pltpu.VMEM((GROUP, HALF, COLS), BF16),
            pltpu.VMEM((2, GROUP, HALF, COLS), BF16),
            pltpu.VMEM((2, GROUP, HALF, COLS), BF16),
            pltpu.VMEM((2, GROUP, 8, BS), F32),
            pltpu.VMEM((CELLS, 128), F32),
            pltpu.VMEM((CELLS, 128), F32),
            pltpu.VMEM((WIN, CELLS), F32),
            pltpu.VMEM((WROWS, CELLS), F32),
            pltpu.VMEM((NCOND * BS, COLS), BF16),
            pltpu.VMEM((CELLS, STATIONS), BF16),
            pltpu.VMEM((STATIONS, COLS), BF16),
            dma,
            dma, dma((3 + ZS,)), dma, dma,
            dma, dma((A_SEMS,)), dma, dma((B_SEMS,)),
            dma, dma((A_SEMS,)), dma, dma((B_SEMS,)), dma, dma((B_SEMS,)),
            dma, dma((ZS,)), dma, dma((XS,)), dma, dma,
        ],
        compiler_params=pltpu.CompilerParams(
            collective_id=0, has_side_effects=True, vmem_limit_bytes=56 * 1024 * 1024
        ),
    )(cond, tiles, sv, weights, factor, xy, cells, rain)
    return thresholds, share.reshape(-1)


def solution(mesh):
    both = ("cont", "dev")
    placed = (
        P(both, None, None),
        P(both, None, None),
        P(both, None, None),
        P(both, None),
        P(both, None, None),
        P(None, both),
        P(both, None),
        P(None, both),
    )
    return jax.shard_map(
        per_device,
        mesh=mesh,
        in_specs=placed,
        out_specs=(P(both, None), P(both)),
        check_vma=False,
    )
```

time: 313 us -> 100 us (0.32)
  waiting for transfers between devices: 158 us -> 0 us
  Pallas kernels: 0 us -> 91.1 us
  local copies, waits for them, and re-layouts: 53.3 us -> 6.85 us
  blocking collectives: 35.2 us -> 0 us
  matrix products: 31.3 us -> 0 us
  between operations: 14.2 us -> 0.65 us
  other arithmetic: 11.5 us -> 0 us
  starting transfers between devices: 8.09 us -> 0 us
    all_gather x2 -> x0, waiting for transfers between devices: 157 us -> none  [the longest x1 80.7 us: per_device(): continent_values = lax.all_gather(station_values, 'dev', axis=0, tiled=True)]
    pallas_call x0 -> x1, Pallas kernels: none -> 91.1 us  [per_device(): pl.pallas_call(kernel, out_shape=(jax.ShapeDtypeStruct((CELLS, DAYS), BF1...]
    all_gather x1 -> x0, blocking collectives: 35.2 us -> none  [per_device(): lax.all_gather(station_xy, 'dev', axis=0, tiled=True)]
    dot_general x6 -> x0, matrix products: 31.3 us -> none  [the longest x4 29.1 us: one_tile(): jnp.dot(weights_tile, chosen, preferred_element_type=jnp.float32)]
    gather x9 -> x0, local copies, waits for them, and re-layouts: 19.5 us -> none  [the longest x4 14.7 us: one_tile(): jnp.take(cand_weights, tile_slots, axis=0)]
    while x2 -> x0, local copies, waits for them, and re-layouts: 13.1 us -> none  [per_device(): threshold_all, share_all = lax.map(one_tile, (slots, cell_grid, rain_grid))]
    ppermute x2 -> x0, starting transfers between devices: 8.02 us -> none  [from_behind(): return lax.ppermute(block, axis, route)]
    concatenate x2 -> x0, other arithmetic: 6.62 us -> none  [the longest x1 6.57 us: per_device(): cand_weights = jnp.concatenate([prev_weights, own_weights], axis=0)]
  transfers between devices with their start and end apart: 4 -> 0, of which waited for: 2 -> 0; matrix products, arithmetic and copies ran while one was open for 1% -> 0% of each run, Pallas kernels for 0% -> 0%
where the time goes in v1:
time: 100 us; the launch traced here: 98.6 us
  Pallas kernels  91.1 us (91%)
  local copies, waits for them, and re-layouts  6.85 us (7%)
    pallas_call x1, Pallas kernels, per_device(): pl.pallas_call(kernel, out_shape=(jax.ShapeDtypeStruct((CELLS, DAYS), BF1...  91.1 us
    unnamed x5, local copies, waits for them, and re-layouts  6.85 us

profile of v1, /device:TPU:1, one launch (start us, length us, event | category | flops | bytes accessed | tf_op | source)
XLA Modules:
  0.0 98.6 jit_solution(15499328437933108409)
XLA Ops:
  0.6 1.6 %copy.10.sv = bf16[1,128,366]{2,1,0:T(8,128)(2,1)} copy(bf16[1,128,366]{1,2,0:T(8,128)(2,1)} %param.8) | data formatting | bytes 187392 | tf_op args[0]
  2.3 91.1 %shard_map.95 = (bf16[4096,366]{1,0:T(8,128)(2,1)}, f32[1,4096]{1,0:T(1,128)}) custom-call(s32[1,4]{1,0:T(1,128)} %cond.1, s32[4,16]{1,0:T(4,128)} %tiles.1, bf16[1,128,366]{2,1,0:T(8,128)(2,1)} %copy.10.sv, bf16[1,128,512]{2,1,0:T(8,128)(2,1)} %weights.1, bf16[1,128,128]{2,1,0:T(8,128)(2,1)} %factor.1, bf16[1,2,128]{2,1,0:T(2,128)(2,1)} %xy.1, ...), custom_call_target="tpu_custom_call" | custom-call | tf_op jit(solution)/shard_map/pallas_call | solution.py:447
  93.3 0.0 copy-start
  93.3 4.6 %copy.11 = bf16[4096,366]{0,1:T(8,128)(2,1)} copy(bf16[4096,366]{1,0:T(8,128)(2,1)} %get-tuple-element.6) | data formatting | bytes 5996544
  97.9 0.0 copy-done
  97.9 0.6 copy.13
Async XLA Ops:
  93.3 4.6 %copy-start = (f32[1,4096]{1,0:T(1,128)S(1)}, f32[1,4096]{1,0:T(1,128)}, u32[]{:S(2)}) copy-start(f32[1,4096]{1,0:T(1,128)} %get-tuple-element.5) | copy-start | bytes 49156
